TPU v7x, 512 devices: a whole 4x4x16 slice. The times are simulated.
512 devices in a mesh: dp: 64 (over y, z), segment: 2 (over core), mp: 4 (over x).
Axes of the slice: x: 4, y: 4, z: 16, core: 2. Of those that a mesh axis runs over, the one named last changes fastest.
Arguments:
- hidden: bfloat16 [2, 512, 4096], P('segment', ('dp', 'mp')), may hold values from -6 to 6
- gain: float32 [4096], replicated, may hold values from 0.5 to 1.5
- head: bfloat16 [4096, 131072], P('segment', ('dp', 'mp')), may hold values from -0.09375 to 0.09375
- queries: bfloat16 [8, 131072], P(None, ('dp', 'mp')), may hold values from -48 to 48
- doc_spans: int32 [8], replicated, may hold values from 1 to 4, as said below
- labels: int32 [8], replicated, may hold values from 0 to 7
Outputs:
- grad_head: bfloat16 [4096, 131072], P('segment', ('dp', 'mp'))
- loss: float32 [], replicated
Inputs may be any that keep to these rules, and one draw needn't show every extreme that they name: `doc_spans`: the counts sum to 16; documents own consecutive spans in order; at least two documents have 4 spans.
All inputs are finite; a program needn't handle non-finite values.
Results may differ from a plain program's by a relative error of at most 0.008.
Values may be sent and summed in bfloat16 or wider, within the bound.
A program may use at most 64 MiB of HBM per device.

v0:
```python
import math

import jax
import jax.numpy as jnp
from jax import lax
from jax.sharding import PartitionSpec as P

V_DEV = 512
CH_MB = 8
NDOC = 8


def saturate(logits):
    return jnp.log1p(jax.nn.softplus(logits))


def slope(logits):
    return jax.nn.sigmoid(logits) / (1.0 + jax.nn.softplus(logits))


def row_norm(hidden, gain):
    values = hidden.astype(jnp.float32)
    mean_sq = jnp.mean(values * values, axis=-1, keepdims=True)
    return (values * lax.rsqrt(mean_sq + 1e-05) * gain).astype(jnp.bfloat16)


def owned_by(span_ids, bounds):
    inside = (span_ids[:, None] >= bounds[None, :-1]) & (span_ids[:, None] < bounds[None, 1:])
    return inside.astype(jnp.float32)


def shards(hidden, gain, head, queries, doc_spans, labels):
    width_dp = lax.axis_size("dp")
    width_mp = lax.axis_size("mp")
    segments = lax.axis_size("segment")
    vocab = V_DEV * width_dp * width_mp
    rows_here = hidden.shape[1]
    tok_mb = rows_here * width_dp * width_mp
    span = tok_mb // CH_MB
    micro_index = lax.axis_index("segment")
    normed = row_norm(hidden, gain)
    head_full = lax.all_gather(head, "segment", axis=0, tiled=True)
    bounds = jnp.concatenate([jnp.zeros((1,), jnp.int32), jnp.cumsum(doc_spans)])
    query_values = queries.astype(jnp.float32)
    scale = 1.0 / (math.sqrt(vocab) * span)

    def doc_table(count):
        span_ids = (micro_index * tok_mb + jnp.arange(count, dtype=jnp.int32)) // span
        return owned_by(span_ids, bounds)

    table = doc_table(tok_mb)
    rows = lax.all_gather(normed, ("dp", "mp"), axis=1, tiled=True)[0]
    block = jnp.dot(rows, head_full, preferred_element_type=jnp.float32)
    local_table = doc_table(rows.shape[0])
    pooled_now = jnp.dot(local_table.T, saturate(block), precision=lax.Precision.HIGHEST)
    pooled = pooled_now
    pooled = lax.psum(pooled, "segment")
    terms = jnp.dot(query_values, pooled.T, precision=lax.Precision.HIGHEST)
    scores = lax.psum(terms, ("dp", "mp")) * scale
    row_top = jnp.max(scores, axis=1, keepdims=True)
    log_total = row_top + jnp.log(jnp.sum(jnp.exp(scores - row_top), axis=1, keepdims=True))
    picks = (labels[:, None] == jnp.arange(NDOC, dtype=jnp.int32)[None, :]).astype(jnp.float32)
    loss = jnp.sum(log_total[:, 0] - jnp.sum(scores * picks, axis=1))
    score_grad = jnp.exp(scores - log_total) - picks
    pooled_grad = scale * jnp.dot(score_grad.T, query_values, precision=lax.Precision.HIGHEST)
    token_grad = jnp.dot(table, pooled_grad, precision=lax.Precision.HIGHEST)
    grad_scale = math.sqrt(vocab) * span / math.sqrt(segments * tok_mb)
    logit_grad = (token_grad * slope(block) * grad_scale).astype(jnp.bfloat16)
    rows = lax.all_gather(normed, ("dp", "mp"), axis=1, tiled=True)[0]
    summed = lax.dot_general(
        rows, logit_grad, (((0,), (0,)), ((), ())), preferred_element_type=jnp.float32
    )
    grad_head = lax.psum_scatter(
        summed.astype(jnp.bfloat16), "segment", scatter_dimension=0, tiled=True
    )
    return (grad_head, loss)


def solution(mesh):
    return jax.shard_map(
        shards,
        mesh=mesh,
        in_specs=(
            P("segment", ("dp", "mp"), None),
            P(),
            P("segment", ("dp", "mp")),
            P(None, ("dp", "mp")),
            P(),
            P(),
        ),
        out_specs=(P("segment", ("dp", "mp")), P()),
        check_vma=False,
    )
```

profile of v0, /device:TPU:1, one launch (start us, length us, event | category | flops | bytes accessed | tf_op | source)
XLA Modules:
  0.0 1000.5 jit_solution(7330918718881482748)
XLA Ops:
  7.2 0.0 copy-start
  7.2 0.0 all-gather.5.cloned.1.call-start
  7.2 0.7 all-gather.5.cloned.1.call-update
  7.9 0.0 all-gather.3.cloned.1.call-start
  8.0 0.9 fusion.16
  8.8 0.8 fusion.18
  9.7 0.6 copy.10
  10.3 0.0 all-gather.3.cloned.1.call-update
  10.3 0.0 reduce-scatter.2.cloned.1.call-start
  10.4 0.8 reduce-window.8
  11.2 0.1 pad_add_fusion
  11.3 0.0 copy-start.1
  11.3 29.7 %all-gather.5.cloned.1.call-done = bf16[4096,512]{1,0:T(8,128)(2,1)} async-done(((bf16[2048,512]{1,0:T(8,128)(2,1)}), bf16[4096,512]{1,0:T(8,128)(2,1)}) %all-gather.5.cloned.1.call-update) | async-done | bytes 4194320 | tf_op jit(solution)/shard_map/all_gather | solution.py:42
  41.0 216.8 %all-gather.3.cloned.1.call-done = bf16[1,512,4096]{2,0,1:T(2,128)(2,1)} async-done(((bf16[1,2,4096]{2,0,1:T(2,128)(2,1)}), bf16[1,512,4096]{2,0,1:T(2,128)(2,1)}) %all-gather.3.cloned.1.call-update) | async-done | bytes 4194320 | tf_op jit(solution)/shard_map/all_gather | solution.py:69
  257.8 9.3 fusion.1
  267.1 1.4 fusion.7
  268.5 11.3 %psum.14 = f32[8,512]{1,0:T(8,128)S(1)} all-reduce(f32[8,512]{1,0:T(8,128)S(1)} %fusion.7), channel_id=1, replica_groups=mesh['dp'=64,'segment'=2,'mp'=4] {'segment'}, use_global_device_ids=true, to_apply=%region_2.3 | all-reduce | flops 4096 | bytes 32768 | tf_op jit(solution)/shard_map/psum | solution.py:57
  279.7 0.0 copy-done
  279.7 0.1 convolution_bitcast_fusion
  279.9 577.1 %psum.15 = f32[8,8]{0,1:T(8,128)S(1)} all-reduce(f32[8,8]{0,1:T(8,128)S(1)} %convolution_bitcast_fusion), channel_id=1, replica_groups=mesh['dp'=64,'segment'=2,'mp'=4] {'dp','mp'}, use_global_device_ids=true, to_apply=%region_3.4 | all-reduce | flops 64 | bytes 512 | tf_op jit(solution)/shard_map/psum | solution.py:59
  857.0 0.0 copy-done.1
  857.0 0.6 subtract_reduce_fusion
  857.6 0.1 convolution_multiply_fusion.1
  857.7 1.4 fusion.6
  859.1 14.9 %convolution_convert_fusion = bf16[4096,512]{1,0:T(8,128)(2,1)} fusion(bf16[512,512]{1,0:T(8,128)(2,1)S(1)} %fusion.6, bf16[1,512,4096]{2,0,1:T(2,128)(2,1)} %all-gather.3.cloned.1.call-done), kind=kOutput, calls=%fused_computation | convolution fusion | flops 2149580800 | bytes 8912896 | tf_op jit(solution)/shard_map/dot_general | solution.py:70
  874.0 0.0 reduce-scatter.2.cloned.1.call-update
  874.0 119.9 %reduce-scatter.2.cloned.1.call-done = bf16[2048,512]{1,0:T(8,128)(2,1)} async-done(((bf16[4096,512]{1,0:T(8,128)(2,1)}), bf16[2048,512]{1,0:T(8,128)(2,1)}) %reduce-scatter.2.cloned.1.call-update) | async-done | bytes 2097168 | tf_op jit(solution)/shard_map/reduce_scatter | solution.py:73
  (4 shorter events, 0.1 us)
Async XLA Ops:
  7.2 272.6 %copy-start = (bf16[8,512]{1,0:T(8,128)(2,1)S(1)}, bf16[8,512]{1,0:T(8,128)(2,1)}, u32[]{:S(2)}) copy-start(bf16[8,512]{1,0:T(8,128)(2,1)} %param.9) | copy-start | bytes 24580
  7.2 33.8 %all-gather.5.cloned.1.call-start = ((), (), s32[]{:S(2)}) async-start(), calls=%async_computation.2 | async-start | bytes 6291456 | tf_op jit(solution)/shard_map/all_gather | solution.py:42
  7.9 249.9 %all-gather.3.cloned.1.call-start = ((), (), s32[]{:S(2)}) async-start(), calls=%async_computation.1 | async-start | bytes 8421376 | tf_op jit(solution)/shard_map/all_gather | solution.py:69
  10.3 983.7 %reduce-scatter.2.cloned.1.call-start = ((), (), s32[]{:S(2)}) async-start(), calls=%async_computation.3 | async-start | bytes 6291456 | tf_op jit(solution)/shard_map/reduce_scatter | solution.py:73
  11.3 845.7 %copy-start.1 = (s32[8]{0:T(128)S(1)}, s32[8]{0:T(128)}, u32[]{:S(2)}) copy-start(s32[8]{0:T(128)} %param.11) | copy-start | bytes 100
Sparse Core Ops, SparseCore 0:
  10.1 30.8 all-gather.4
  46.2 211.6 all-gather.2
  874.2 119.7 reduce-scatter.1
where the time goes:
time: 1000 us
  blocking collectives  588 us (59%)
  waiting for transfers between devices  367 us (37%)
  matrix products  27.1 us (3%)
  between operations  13.8 us (1%)
    psum x1, blocking collectives, shards(): scores = lax.psum(terms, ('dp', 'mp')) * scale  577 us
    all_gather x1, waiting for transfers between devices, shards(): rows = lax.all_gather(normed, ('dp', 'mp'), axis=1, tiled=True)[0]  217 us
    reduce_scatter x1, waiting for transfers between devices, shards(): lax.psum_scatter(summed.astype(jnp.bfloat16), 'segment', scatter_dimensio...  120 us
    all_gather x1, waiting for transfers between devices, shards(): head_full = lax.all_gather(head, 'segment', axis=0, tiled=True)  29.7 us
  transfers between devices with their start and end apart: 3, of which 3 were waited for; matrix products, arithmetic and copies ran while one was open for 0% of the time, Pallas kernels for 0%

commit v1 on v0

v1 whole, which is shorter than its diff:
```python
import functools
import math

import jax
import jax.numpy as jnp
from jax import lax
from jax.experimental import pallas as pl
from jax.experimental.pallas import tpu as pltpu
from jax.sharding import PartitionSpec as P

MESH = pl.DeviceIdType.MESH
NX, NY, NZ = 4, 4, 16
V_DEV = 512
NDOC = 8
NQ = 8
SPANS = 16
SPAN = 64
VOCAB = 131072
TOKENS = 1024
D = 4096
DH = D // 2
LANES = 128

WA, WB, WQ = 768, 768, 128
A_CHUNKS = ((0, 384), (384, 384))
B_AT, B_WIDTH = WA, WB + WQ
B_HALVES = ((WA, 512), (WA + 512, B_WIDTH - 512))
C_AT = WA + WB
assert C_AT + 4 * WQ == DH

LAST = 11


def wrap(i, n):
    return lax.rem(i + 2 * n, n)


def kernel(
    hidden, gain, head, queries, doc_spans, labels,
    out, loss,
    ysend, yland, xs, hs, mine, sent, got, slopes, pool, xt, lg, outs, spg,
    ar0, ar1, ar2, ar3,
    h_sem, o_sem,
    p1_s, p1_r, y_s, y_r, rb_s, rb_r, ra_s, ra_r, x_s, x_r, pp_s, pp_r, sl_s, sl_r,
    a1_s, a1_r, a2_s, a2_r, a3_s, a3_r,
):
    x = lax.axis_index("mp")
    s = lax.axis_index("segment")
    dp = lax.axis_index("dp")
    y = dp // NZ
    z = lax.rem(dp, NZ)

    def dev(dx=0, dy=0, dz=0, ds=0):
        return (
            wrap(y + dy, NY) * NZ + wrap(z + dz, NZ),
            wrap(s + ds, 2),
            wrap(x + dx, NX),
        )

    def copy(src, dst, s_sem, r_sem, device):
        return pltpu.make_async_remote_copy(
            src, dst, s_sem, r_sem, device, device_id_type=MESH
        )

    near = [(dx, ds) for dx in range(NX) for ds in range(2) if dx or ds]
    barrier = pltpu.get_barrier_semaphore()
    peers = [dev(dx=dx, ds=ds) for dx, ds in near]
    peers += [dev(dy=dy) for dy in range(1, NY)]
    peers += [dev(dz=1), dev(dz=-1)]
    for p in peers:
        pl.semaphore_signal(barrier, inc=1, device_id=p, device_id_type=MESH)

    def h_copies():
        yield pltpu.make_async_copy(head.at[pl.ds(0, C_AT)], hs.at[pl.ds(0, C_AT)], h_sem.at[0])
        for r in range(NX):
            at = pl.multiple_of(C_AT + wrap(x + r, NX) * WQ, WQ)
            yield pltpu.make_async_copy(
                head.at[pl.ds(at, WQ)], hs.at[pl.ds(C_AT + r * WQ, WQ)], h_sem.at[1 + r]
            )

    for c in h_copies():
        c.start()

    values = hidden[0].astype(jnp.float32)
    mean_sq = jnp.mean(values * values, axis=-1, keepdims=True)
    normed = (values * lax.rsqrt(mean_sq + 1e-05) * gain[...]).astype(jnp.bfloat16)
    normed = normed.astype(jnp.float32)
    for k in range(D // LANES):
        ysend[k // 16, :, k % 16, :] = normed[:, k * LANES : (k + 1) * LANES]
    pool[...] = jnp.zeros_like(pool)

    pl.semaphore_wait(barrier, len(peers))

    def p1(i, dx, ds, landing):
        return copy(
            ysend.at[wrap(s + ds, 2)],
            yland.at[pl.ds(landing * 2, 2)],
            p1_s.at[i], p1_r.at[i], dev(dx=dx, ds=ds),
        )

    for i, (dx, ds) in enumerate(near):
        p1(i, dx, ds, s * NX + x).start()
    yland[pl.ds((s * NX + x) * 2, 2)] = ysend[s]
    for i, (dx, ds) in enumerate(near):
        p1(i, dx, ds, wrap(s + ds, 2) * NX + wrap(x - dx, NX)).wait_recv()
    for k in range(C_AT // LANES):
        xs[z, y, :, k * LANES : (k + 1) * LANES] = yland[:, k, :].astype(jnp.bfloat16)
    for xx in range(NX):

        @pl.when(x == xx)
        def _():
            for r in range(NX):
                k = C_AT // LANES + (xx + r) % NX
                at = C_AT + r * WQ
                xs[z, y, :, at : at + WQ] = yland[:, k, :].astype(jnp.bfloat16)

    def zed(k, d):
        return wrap(z - k, NZ) if d == 0 else wrap(z + k, NZ)

    def ring_b(k, d, zb, at=B_AT, width=B_WIDTH):
        ref = xs.at[zb, y, :, pl.ds(at, width)]
        return copy(ref, ref, rb_s.at[d, k], rb_r.at[d, k], dev(dz=1 - 2 * d))

    def ring_a(k, d, c, zb):
        ref = xs.at[zb, :, :, pl.ds(*A_CHUNKS[c])]
        return copy(ref, ref, ra_s.at[d, k, c], ra_r.at[d, k, c], dev(dz=1 - 2 * d))

    def relay_y(i, dy, zb, yb, at=B_AT, width=B_WIDTH):
        ref = xs.at[zb, yb, :, pl.ds(at, width)]
        return copy(ref, ref, y_s.at[i, dy - 1], y_r.at[i, dy - 1], dev(dy=dy))

    def relay_x(i, dx, zb):
        return copy(
            xs.at[zb, :, :, pl.ds(C_AT, WQ)],
            xs.at[zb, :, :, pl.ds(C_AT + (NX - dx) * WQ, WQ)],
            x_s.at[i, dx - 1], x_r.at[i, dx - 1], dev(dx=dx),
        )

    def partial(k):
        return copy(sent.at[k], got.at[k], pp_s.at[k], pp_r.at[k], dev(ds=1))

    def zown(k):
        return lax.rem(z + jnp.where(s == 0, NZ - k, k), NZ)

    def zother(k):
        return lax.rem(z + jnp.where(s == 0, k, NZ - k), NZ)

    def slope_copy(k, zb):
        return copy(slopes.at[zb], slopes.at[zb], sl_s.at[k], sl_r.at[k], dev(ds=1))

    def rows_of(zb):
        return xs[zb].reshape(NY * 16, DH)

    for d in range(2):
        ring_b(1, d, z).start()
    for dy in range(1, NY):
        relay_y(0, dy, z, y, 0, DH).start()
    for dy in range(1, NY):
        relay_y(0, dy, z, wrap(y - dy, NY), 0, DH).wait_recv()
    for c in range(2):
        for d in range(2):
            ring_a(1, d, c, z).start()
    for c in h_copies():
        c.wait()
    product = jnp.dot(rows_of(z), hs[...], preferred_element_type=jnp.float32)
    mine[0] = product
    sent[0] = product
    partial(0).start()

    def step(k, carry):
        @pl.when(k <= 7)
        def _():
            for d in range(2):
                ring_b(k, d, zed(k, d)).wait_recv()

            @pl.when(k < 7)
            def _():
                for d in range(2):
                    ring_b(k + 1, d, zed(k, d)).start()

            @pl.when(k == 7)
            def _():
                for d in range(2):
                    ring_b(8, d, zed(7, d), *B_HALVES[d]).start()

            for d in range(2):
                for dy in range(1, NY):
                    relay_y(2 * k - 1 + d, dy, zed(k, d), y).start()
            for c in range(2):
                for d in range(2):
                    ring_a(k, d, c, zed(k, d)).wait_recv()

                    @pl.when((k < 7) | (c == d))
                    def _():
                        ring_a(k + 1, d, c, zed(k, d)).start()

        @pl.when(k == 8)
        def _():
            zb = zed(8, 0)
            for d in range(2):
                ring_b(8, d, zb, *B_HALVES[d]).wait_recv()
            for dy in range(1, NY):
                relay_y(15, dy, zb, y).start()
            for d in range(2):
                ring_a(8, d, d, zb).wait_recv()

        @pl.when((k >= 2) & (k <= 9))
        def _():
            j = k - 1
            for d in range(2):

                @pl.when((j <= 7) | (d == 0))
                def _():
                    i = 2 * j - 1 + d
                    zb = zed(j, d)
                    for dy in range(1, NY):
                        relay_y(i, dy, zb, wrap(y - dy, NY)).wait_recv()
                    for dx in range(1, NX):
                        relay_x(i, dx, zb).start()

        @pl.when((k >= 3) & (k <= 9))
        def _():
            j = k - 2
            for d in range(2):
                for dx in range(1, NX):
                    relay_x_wait(2 * j - 1 + d, dx, zed(j, d))
            both = jnp.concatenate([rows_of(zown(j)), rows_of(zother(j))], axis=0)
            product = jnp.dot(both, hs[...], preferred_element_type=jnp.float32)
            mine[j] = product[: NY * 16]
            sent[j] = product[NY * 16 :]
            partial(j).start()

        @pl.when(k == 10)
        def _():
            zb = zed(8, 0)
            for dx in range(1, NX):
                relay_x_wait(15, dx, zb)
            product = jnp.dot(rows_of(zb), hs[...], preferred_element_type=jnp.float32)
            mine[8] = product
            sent[8] = product
            partial(8).start()

        @pl.when(k >= 3)
        def _():
            j = k - 3
            zb = zown(j)
            late = jnp.where(zb >= NZ // 2, 1, 0)
            counts = (j > 0) & (j < 8) | (j == 0) & (s == 0) | (j == 8) & (s == 1)
            weight = jnp.where(counts, 1.0, 0.0).astype(jnp.float32)
            partial(j).wait_recv()
            for yb in range(NY):
                rows = pl.ds(yb * 16, 16)
                logits = mine[j, rows, :] + got[j, rows, :]
                small = jnp.exp(-jnp.abs(logits))
                soft = jnp.maximum(logits, 0.0) + jnp.log1p(small)
                pool[late, yb] += weight * jnp.log1p(soft)
                top = jnp.where(logits >= 0.0, 1.0, small)
                slope = top / ((1.0 + small) * (1.0 + soft))
                slopes[zb, rows, :] = slope.astype(jnp.bfloat16)

            @pl.when((j > 0) & (j < 8))
            def _():
                slope_copy(j, zb).start()

        return carry

    def relay_x_wait(i, dx, zb):
        ref = xs.at[zb, :, :, pl.ds(C_AT + (NX - dx) * WQ, WQ)]
        copy(ref, ref, x_s.at[i, dx - 1], x_r.at[i, dx - 1], dev(dx=dx)).wait_recv()

    lax.fori_loop(1, LAST + 1, step, 0)

    lane = lax.broadcasted_iota(jnp.int32, (NQ, LANES), 1)
    row = lax.broadcasted_iota(jnp.int32, (NQ, LANES), 0)
    query = queries[...].astype(jnp.float32)
    terms = jnp.zeros((NQ, LANES), jnp.float32)
    for late in range(2):
        for yb in range(NY):
            for m in range(2):
                total = jnp.sum(pool[late, yb, m * 8 : (m + 1) * 8, :], axis=0, keepdims=True)
                term = jnp.sum(query * total, axis=1, keepdims=True)
                terms = jnp.where(lane == m * 8 + yb * 2 + late, term, terms)

    def transpose(c, carry):
        at = pl.multiple_of(c * LANES, LANES)
        block = xs[:, :, :, pl.ds(at, LANES)].reshape(TOKENS, LANES)
        xt[pl.ds(at, LANES), :] = block.T
        return carry

    ar0[...] = terms
    to_core = copy(ar0, ar1, a1_s, a1_r, dev(ds=1))
    to_core.start()
    to_core.wait_recv()
    chip = terms + ar1[...]
    ar0_xy = ar2.at[x * NY + y]
    ar2[x * NY + y] = chip

    def to_xy(i):
        return copy(ar0_xy, ar0_xy, a2_s.at[i], a2_r.at[i], dev(dx=i // NY, dy=lax.rem(i, NY)))

    def from_xy(i):
        ref = ar2.at[wrap(x - i // NY, NX) * NY + wrap(y - lax.rem(i, NY), NY)]
        return copy(ref, ref, a2_s.at[i], a2_r.at[i], dev())

    def start_xy(i, carry):
        to_xy(i).start()
        return carry

    def wait_xy(i, carry):
        from_xy(i).wait_recv()
        return carry

    lax.fori_loop(1, NX * NY, start_xy, 0)
    lax.fori_loop(0, 6, transpose, 0)
    lax.fori_loop(1, NX * NY, wait_xy, 0)
    plane = jnp.zeros((NQ, LANES), jnp.float32)
    for i in range(NX * NY):
        plane += ar2[i]
    ar3[z] = plane
    ar_z = ar3.at[z]

    def to_z(i):
        return copy(ar_z, ar_z, a3_s.at[i], a3_r.at[i], dev(dz=i))

    def from_z(i):
        ref = ar3.at[wrap(z - i, NZ)]
        return copy(ref, ref, a3_s.at[i], a3_r.at[i], dev())

    def start_z(i, carry):
        to_z(i).start()
        return carry

    def wait_z(i, carry):
        from_z(i).wait_recv()
        return carry

    lax.fori_loop(1, NZ, start_z, 0)
    lax.fori_loop(6, DH // LANES, transpose, 0)

    def wait_step(k, carry):
        slope_copy(k, zother(k)).wait_recv()
        slope_copy(k, zown(k)).wait_send()
        for d in range(2):
            ring_b(k, d, z).wait_send()
            for c in range(2):
                ring_a(k, d, c, z).wait_send()
            for o in range(1, NY):
                relay_y(2 * k - 1 + d, o, z, y).wait_send()
                relay_x(2 * k - 1 + d, o, z).wait_send()
        partial(k).wait_send()
        return carry

    lax.fori_loop(1, 8, wait_step, 0)
    for d in range(2):
        ring_b(8, d, z, *B_HALVES[d]).wait_send()
        ring_a(8, d, d, z).wait_send()
    for o in range(1, NY):
        relay_y(0, o, z, y, 0, DH).wait_send()
        relay_y(15, o, z, y).wait_send()
        relay_x(15, o, z).wait_send()
    partial(0).wait_send()
    partial(8).wait_send()
    for i, (dx, ds) in enumerate(near):
        p1(i, dx, ds, 0).wait_send()
    to_core.wait_send()

    def sent_xy(i, carry):
        to_xy(i).wait_send()
        return carry

    lax.fori_loop(1, NX * NY, sent_xy, 0)
    lax.fori_loop(1, NZ, wait_z, 0)
    whole = jnp.zeros((NQ, LANES), jnp.float32)
    for i in range(NZ):
        whole += ar3[i]

    masks = []
    first = jnp.int32(0)
    scores = jnp.zeros((NQ, LANES), jnp.float32)
    for d in range(NDOC):
        after = first + doc_spans[d]
        masks.append((lane >= first) & (lane < after))
        term = jnp.sum(jnp.where(masks[d], whole, 0.0), axis=1, keepdims=True)
        scores = jnp.where(lane == d, term, scores)
        first = after
    scores = scores * (1.0 / (math.sqrt(VOCAB) * SPAN))
    valid = lane < NDOC
    row_top = jnp.max(jnp.where(valid, scores, -jnp.inf), axis=1, keepdims=True)
    total = jnp.sum(jnp.where(valid, jnp.exp(scores - row_top), 0.0), axis=1, keepdims=True)
    log_total = row_top + jnp.log(total)
    picks = jnp.zeros((NQ, LANES), jnp.float32)
    for q in range(NQ):
        picks = jnp.where((row == q) & (lane == labels[q]), 1.0, picks)
    picked = jnp.sum(scores * picks, axis=1, keepdims=True)
    loss[...] = jnp.sum(log_total - picked, axis=0, keepdims=True)
    grad = jnp.where(valid, jnp.exp(scores - log_total), 0.0) - picks
    grad = grad * (1.0 / math.sqrt(TOKENS))
    by_span = jnp.zeros((NQ, LANES), jnp.float32)
    for d in range(NDOC):
        column = jnp.sum(jnp.where(lane == d, grad, 0.0), axis=1, keepdims=True)
        by_span = jnp.where(masks[d], column, by_span)
    for i in range(SPANS):
        spg[i : i + 1, :] = jnp.sum(by_span[:, i : i + 1] * query, axis=0, keepdims=True)

    for late in range(2):

        def to_lg(k, carry, late=late):
            zb = late * (NZ // 2) + k
            for yb in range(NY):
                slope = slopes[zb, yb * 16 : (yb + 1) * 16, :].astype(jnp.float32)
                parts = [
                    slope[m * 8 : (m + 1) * 8] * spg[m * 8 + yb * 2 + late, :][None, :]
                    for m in range(2)
                ]
                at = pl.multiple_of(zb * 64 + yb * 16, 16)
                lg[pl.ds(at, 16), :] = jnp.concatenate(parts, axis=0).astype(jnp.bfloat16)
            return carry

        lax.fori_loop(0, NZ // 2, to_lg, 0)

    def out_copy(b):
        quarter = C_AT // WQ + wrap(x + b, NX)
        at = pl.multiple_of(jnp.where(b < C_AT // WQ, b, quarter) * WQ, WQ)
        here = pl.multiple_of(b * WQ, WQ)
        return pltpu.make_async_copy(outs.at[pl.ds(here, WQ)], out.at[pl.ds(at, WQ)], o_sem.at[b])

    tile = 256

    def to_out(t, carry):
        at = pl.ds(pl.multiple_of(t * tile, tile), tile)
        block = jnp.dot(xt[at, :], lg[...], preferred_element_type=jnp.float32)
        outs[at, :] = block.astype(jnp.bfloat16)
        for h in range(tile // WQ):
            out_copy(t * (tile // WQ) + h).start()
        return carry

    lax.fori_loop(0, DH // tile, to_out, 0)

    def sent_z(i, carry):
        to_z(i).wait_send()
        return carry

    lax.fori_loop(1, NZ, sent_z, 0)

    def out_wait(b, carry):
        out_copy(b).wait()
        return carry

    lax.fori_loop(0, DH // WQ, out_wait, 0)


def shards(hidden, gain, head, queries, doc_spans, labels):
    dma = pltpu.SemaphoreType.DMA
    f32, bf16 = jnp.float32, jnp.bfloat16
    vmem = pl.BlockSpec(memory_space=pltpu.VMEM)
    smem = pl.BlockSpec(memory_space=pltpu.SMEM)
    hbm = pl.BlockSpec(memory_space=pl.ANY)
    grad_head, loss = pl.pallas_call(
        kernel,
        name="splade_head",
        out_shape=(
            jax.ShapeDtypeStruct((DH, V_DEV), bf16),
            jax.ShapeDtypeStruct((1, 1), f32),
        ),
        in_specs=[vmem, vmem, hbm, vmem, smem, smem],
        out_specs=(hbm, vmem),
        scratch_shapes=[
            pltpu.VMEM((2, 2, 16, LANES), f32),
            pltpu.VMEM((16, 16, LANES), f32),
            pltpu.VMEM((NZ, NY, 16, DH), bf16),
            pltpu.VMEM((DH, V_DEV), bf16),
            pltpu.VMEM((9, NY * 16, V_DEV), f32),
            pltpu.VMEM((9, NY * 16, V_DEV), f32),
            pltpu.VMEM((9, NY * 16, V_DEV), f32),
            pltpu.VMEM((NZ, NY * 16, V_DEV), bf16),
            pltpu.VMEM((2, NY, 16, V_DEV), f32),
            pltpu.VMEM((DH, TOKENS), bf16),
            pltpu.VMEM((TOKENS, V_DEV), bf16),
            pltpu.VMEM((DH, V_DEV), bf16),
            pltpu.VMEM((SPANS, V_DEV), f32),
            pltpu.VMEM((NQ, LANES), f32),
            pltpu.VMEM((NQ, LANES), f32),
            pltpu.VMEM((NX * NY, NQ, LANES), f32),
            pltpu.VMEM((NZ, NQ, LANES), f32),
            dma((5,)), dma((DH // WQ,)),
            dma((7,)), dma((7,)),
            dma((16, 3)), dma((16, 3)),
            dma((2, 9)), dma((2, 9)),
            dma((2, 9, 2)), dma((2, 9, 2)),
            dma((16, 3)), dma((16, 3)),
            dma((9,)), dma((9,)),
            dma((9,)), dma((9,)),
            dma, dma,
            dma((16,)), dma((16,)),
            dma((16,)), dma((16,)),
        ],
        compiler_params=pltpu.CompilerParams(
            collective_id=0, has_side_effects=True, vmem_limit_bytes=48 * 2**20
        ),
    )(hidden, gain.reshape(1, D), head, queries, doc_spans, labels)
    return (grad_head, loss.reshape(()))


def solution(mesh):
    return jax.shard_map(
        shards,
        mesh=mesh,
        in_specs=(
            P("segment", ("dp", "mp"), None),
            P(),
            P("segment", ("dp", "mp")),
            P(None, ("dp", "mp")),
            P(),
            P(),
        ),
        out_specs=(P("segment", ("dp", "mp")), P()),
        check_vma=False,
    )
```

time: 1000 us -> 94.2 us (0.09)
  blocking collectives: 588 us -> 0 us
  waiting for transfers between devices: 367 us -> 0 us
  Pallas kernels: 0 us -> 84.4 us
  matrix products: 27.1 us -> 0 us
  between operations: 13.8 us -> 2.47 us
    psum x2 -> x0, blocking collectives: 588 us -> none  [the longest x1 577 us: shards(): scores = lax.psum(terms, ('dp', 'mp')) * scale]
    all_gather x2 -> x0, waiting for transfers between devices: 247 us -> none  [the longest x1 217 us: shards(): rows = lax.all_gather(normed, ('dp', 'mp'), axis=1, tiled=True)[0]]
    reduce_scatter x1 -> x0, waiting for transfers between devices: 120 us -> none  [shards(): lax.psum_scatter(summed.astype(jnp.bfloat16), 'segment', scatter_dimensio...]
    pallas_call x0 -> x1, Pallas kernels: none -> 84.4 us  [shards(): pl.pallas_call(kernel, name='splade_head', out_shape=(jax.ShapeDtypeStruc...]
    dot_general x6 -> x0, matrix products: 27.1 us -> none  [the longest x1 14.9 us: shards(): lax.dot_general(rows, logit_grad, (((0,), (0,)), ((), ())), preferred_ele...]
  transfers between devices with their start and end apart: 3 -> 0, of which waited for: 3 -> 0; matrix products, arithmetic and copies ran while one was open for 0% -> 0% of each run, Pallas kernels for 0% -> 0%
where the time goes in v1:
time: 94.2 us; the launch traced here: 93.3 us
  Pallas kernels  84.4 us (90%)
  local copies, waits for them, and re-layouts  6.35 us (7%)
  between operations  2.47 us (3%)
    pallas_call x1, Pallas kernels, shards(): pl.pallas_call(kernel, name='splade_head', out_shape=(jax.ShapeDtypeStruc...  84.4 us
    unnamed x13, local copies, waits for them, and re-layouts  6.35 us

profile of v1, /device:TPU:1, one launch (start us, length us, event | category | flops | bytes accessed | tf_op | source)
XLA Modules:
  0.0 93.3 jit_solution(10342940355951841922)
XLA Ops:
  0.6 0.0 copy-start
  0.6 1.6 %copy-done = bf16[2048,512]{1,0:T(8,128)(2,1)S(1)} copy-done((bf16[2048,512]{1,0:T(8,128)(2,1)S(1)}, bf16[2048,512]{1,0:T(8,128)(2,1)}, u32[]{:S(2)}) %copy-start) | copy-done | bytes 2097176
  2.2 0.0 copy-start.1
  2.2 0.7 copy-done.1
  2.9 0.0 copy-start.2
  2.9 0.7 copy-done.2
  3.7 0.0 copy-start.3
  3.7 0.7 copy-done.3
  4.4 0.0 copy-start.4
  4.4 0.7 copy-done.4
  5.0 0.0 copy-start.5
  5.0 0.7 copy-done.5
  5.7 84.4 %splade_head.1 = (bf16[2048,512]{1,0:T(8,128)(2,1)S(1)}, f32[1,1]{1,0:T(1,128)}) custom-call(bf16[1,2,4096]{2,1,0:T(2,128)(2,1)S(1)} %copy-done.1, f32[1,4096]{1,0:T(1,128)S(1)} %bitcast.2, bf16[2048,512]{1,0:T(8,128)(2,1)S(1)} %copy-done, bf16[8,512]{1,0:T(8,128)(2,1)S(1)} %copy-done.3, s32[8]{0:T(128)S(1)} %copy-done.4, s32[8]{0:T(128)S(1)} %copy-done.5), custom_call_target="tpu_custom_call" | custom-call | tf_op jit(solution)/shard_map/splade_head/pallas_call | solution.py:458
  90.1 1.3 %copy.10 = bf16[2048,512]{1,0:T(8,128)(2,1)} copy(bf16[2048,512]{1,0:T(8,128)(2,1)S(1)} %get-tuple-element.8) | data formatting | bytes 4194304
Async XLA Ops:
  0.6 1.6 %copy-start = (bf16[2048,512]{1,0:T(8,128)(2,1)S(1)}, bf16[2048,512]{1,0:T(8,128)(2,1)}, u32[]{:S(2)}) copy-start(bf16[2048,512]{1,0:T(8,128)(2,1)} %head.1) | copy-start | bytes 6291460
  2.2 0.7 copy-start.1
  2.9 0.7 copy-start.2
  3.7 0.7 copy-start.3
  4.4 0.7 copy-start.4
  5.0 0.7 copy-start.5

commit v2 on v1

v2 whole, which is shorter than its diff:
```python
import functools
import math

import jax
import jax.numpy as jnp
from jax import lax
from jax.experimental import pallas as pl
from jax.experimental.pallas import tpu as pltpu
from jax.sharding import PartitionSpec as P

MESH = pl.DeviceIdType.MESH
NX, NY, NZ = 4, 4, 16
V_DEV = 512
NDOC = 8
NQ = 8
SPANS = 16
ROWS = 128
SPAN = 64
VOCAB = 131072
TOKENS = 1024
D = 4096
DH = D // 2
LANES = 128

WB, WQ = 1024, 256
WHOLE = (0, WB + WQ)
HALVES = ((0, 640), (640, WB + WQ - 640))
C_AT = WB
assert C_AT + 4 * WQ == DH

OWN = 15
STEPS = 4


def wrap(i, n):
    return lax.rem(i + 2 * n, n)


def kernel(
    hidden_at, gain_at, head, queries_at, doc_spans_at, labels_at,
    out, loss,
    hidden, gain, queries, doc_spans, labels,
    ysend, yland, xs, hs, mine, sent, got, slopes, pool, xt, lg, outs, spg,
    ar0, ar1, ar2, ar3,
    in_sem, h_sem, o_sem,
    p1_s, p1_r, y_s, y_r, r_s, r_r, x_s, x_r, pp_s, pp_r, sl_s, sl_r,
    a1_s, a1_r, a2_s, a2_r, a3_s, a3_r,
):
    x = lax.axis_index("mp")
    s = lax.axis_index("segment")
    dp = lax.axis_index("dp")
    y = dp // NZ
    z = lax.rem(dp, NZ)

    def dev(dx=0, dy=0, dz=0, ds=0):
        return (
            wrap(y + dy, NY) * NZ + wrap(z + dz, NZ),
            wrap(s + ds, 2),
            wrap(x + dx, NX),
        )

    def copy(src, dst, s_sem, r_sem, device):
        return pltpu.make_async_remote_copy(
            src, dst, s_sem, r_sem, device, device_id_type=MESH
        )

    inputs = [
        pltpu.make_async_copy(a, b, in_sem.at[i])
        for i, (a, b) in enumerate(
            ((hidden_at, hidden), (gain_at, gain), (queries_at, queries),
             (doc_spans_at, doc_spans), (labels_at, labels))
        )
    ]
    for c in inputs:
        c.start()

    near = [(dx, ds) for dx in range(NX) for ds in range(2) if dx or ds]
    barrier = pltpu.get_barrier_semaphore()
    peers = [dev(dx=dx, ds=ds) for dx, ds in near]
    peers += [dev(dy=dy) for dy in range(1, NY)]
    peers += [dev(dz=dz) for dz in (1, 2, -1, -2)]
    for p in peers:
        pl.semaphore_signal(barrier, inc=1, device_id=p, device_id_type=MESH)

    h_copies = [pltpu.make_async_copy(head.at[pl.ds(0, C_AT)], hs.at[pl.ds(0, C_AT)], h_sem.at[0])]
    for r in range(NX):
        at = pl.multiple_of(C_AT + wrap(x + r, NX) * WQ, WQ)
        h_copies.append(
            pltpu.make_async_copy(
                head.at[pl.ds(at, WQ)], hs.at[pl.ds(C_AT + r * WQ, WQ)], h_sem.at[1 + r]
            )
        )

    inputs[0].wait()
    inputs[1].wait()
    values = hidden[0].astype(jnp.float32)
    mean_sq = jnp.mean(values * values, axis=-1, keepdims=True)
    normed = (values * lax.rsqrt(mean_sq + 1e-05) * gain[...]).astype(jnp.bfloat16)
    normed = normed.astype(jnp.float32)
    for k in range(D // LANES):
        ysend[k // 16, :, k % 16, :] = normed[:, k * LANES : (k + 1) * LANES]

    pl.semaphore_wait(barrier, len(peers))

    def p1(i, dx, ds, landing):
        return copy(
            ysend.at[wrap(s + ds, 2)],
            yland.at[pl.ds(landing * 2, 2)],
            p1_s.at[i], p1_r.at[i], dev(dx=dx, ds=ds),
        )

    for i, (dx, ds) in enumerate(near):
        p1(i, dx, ds, s * NX + x).start()
    for c in h_copies:
        c.start()
    yland[pl.ds((s * NX + x) * 2, 2)] = ysend[s]
    pool[...] = jnp.zeros_like(pool)
    for i, (dx, ds) in enumerate(near):
        p1(i, dx, ds, wrap(s + ds, 2) * NX + wrap(x - dx, NX)).wait_recv()
    for k in range(C_AT // LANES):
        xs[OWN, y, :, k * LANES : (k + 1) * LANES] = yland[:, k, :].astype(jnp.bfloat16)
    for xx in range(NX):

        @pl.when(x == xx)
        def _():
            for r in range(NX):
                for h in range(WQ // LANES):
                    k = (C_AT + (xx + r) % NX * WQ) // LANES + h
                    at = C_AT + r * WQ + h * LANES
                    xs[OWN, y, :, at : at + LANES] = yland[:, k, :].astype(jnp.bfloat16)

    def ring_copy(k, d, piece, src, dst, n, hops, columns=WHOLE):
        a, b = (xs.at[pl.ds(i, n), y, :, pl.ds(*columns)] for i in (src, dst))
        at = 4 * k + 2 * d + piece
        return copy(a, b, r_s.at[at], r_r.at[at], dev(dz=hops if d == 0 else -hops))

    def ring_first(d):
        return [ring_copy(1, d, i, OWN, 8 * d + i, 1, 1 + i) for i in range(2)]

    def ring_middle(d, k):
        at = 8 * d + 2 * (k - 1)
        return [ring_copy(k, d, 0, at - 2, at, 2, 2)]

    def ring_last(d):
        return [
            ring_copy(STEPS, d, 0, 8 * d + 4, 8 * d + 6, 1, 2),
            ring_copy(STEPS, d, 1, 8 * d + 5, 7, 1, 2, HALVES[d]),
        ]

    def start(copies):
        for c in copies:
            c.start()

    def arrive(copies):
        for c in copies:
            c.wait_recv()

    def own_y(dy, yb):
        ref = xs.at[OWN, yb]
        return copy(ref, ref, y_s.at[0, dy - 1], y_r.at[0, dy - 1], dev(dy=dy))

    def relay_y(i, dy, slot, n, yb):
        ref = xs.at[pl.ds(slot, n), yb, :, pl.ds(*WHOLE)]
        return copy(ref, ref, y_s.at[i, dy - 1], y_r.at[i, dy - 1], dev(dy=dy))

    def relay_x(i, dx, slot, n):
        return copy(
            xs.at[pl.ds(slot, n), :, :, pl.ds(C_AT, WQ)],
            xs.at[pl.ds(slot, n), :, :, pl.ds(C_AT + (NX - dx) * WQ, WQ)],
            x_s.at[i, dx - 1], x_r.at[i, dx - 1], dev(dx=dx),
        )

    def partial(k):
        return copy(sent.at[k], got.at[k], pp_s.at[k], pp_r.at[k], dev(ds=1))

    def slope_copy(k, first):
        ref = slopes.at[pl.ds(first, 2)]
        return copy(ref, ref, sl_s.at[k], sl_r.at[k], dev(ds=1))

    def late_of(slot):
        off = jnp.where(slot < 8, NZ - 1 - slot, jnp.where(slot == OWN, 0, slot - 7))
        return jnp.where(lax.rem(z + off, NZ) >= NZ // 2, 1, 0)

    def rows_of(slot):
        return xs[pl.ds(slot, 2)].reshape(ROWS, DH)

    for d in range(2):
        start(ring_first(d))
    for dy in range(1, NY):
        own_y(dy, y).start()

    def on_ring(k):
        @pl.when(k == 1)
        def _():
            for d in range(2):
                arrive(ring_first(d))

        @pl.when((k == 2) | (k == 3))
        def _():
            for d in range(2):
                arrive(ring_middle(d, k))

        @pl.when(k < 3)
        def _():
            for d in range(2):
                start(ring_middle(d, k + 1))

        @pl.when(k == 3)
        def _():
            for d in range(2):
                start(ring_last(d))

        @pl.when(k == STEPS)
        def _():
            for d in range(2):
                arrive(ring_last(d))

    def whole_or_not(k, d, do):
        first = 8 * d + 2 * (k - 1)
        if d == 0:
            do(first, 2)
        else:
            pl.when(k < STEPS)(lambda: do(first, 2))
            pl.when(k == STEPS)(lambda: do(first, 1))

    def step(k, carry):
        @pl.when(k <= STEPS)
        def _():
            on_ring(k)
            for d in range(2):

                def to_y(first, n, d=d):
                    for dy in range(1, NY):
                        relay_y(2 * k - 1 + d, dy, first, n, y).start()

                whole_or_not(k, d, to_y)

        @pl.when((k >= 2) & (k <= STEPS + 1))
        def _():
            j = k - 1
            for d in range(2):

                def y_to_x(first, n, d=d):
                    for dy in range(1, NY):
                        relay_y(2 * j - 1 + d, dy, first, n, wrap(y - dy, NY)).wait_recv()
                    for dx in range(1, NX):
                        relay_x(2 * j - 1 + d, dx, first, n).start()

                whole_or_not(j, d, y_to_x)

        @pl.when((k >= 3) & (k <= STEPS + 2))
        def _():
            j = k - 2
            for d in range(2):

                def from_x(first, n, d=d):
                    for dx in range(1, NX):
                        relay_x(2 * j - 1 + d, dx, first, n).wait_recv()

                whole_or_not(j, d, from_x)

            @pl.when(j == 1)
            def _():
                for c in h_copies:
                    c.wait()

            @pl.when(j == STEPS)
            def _():
                for dy in range(1, NY):
                    own_y(dy, wrap(y - dy, NY)).wait_recv()

            first = 2 * (j - 1)
            other = rows_of(first + 8 * (1 - s))
            sent[j - 1] = jnp.dot(other, hs[...], preferred_element_type=jnp.float32)
            partial(j - 1).start()
            own = rows_of(first + 8 * s)
            mine[j - 1] = jnp.dot(own, hs[...], preferred_element_type=jnp.float32)

        @pl.when(k >= 4)
        def _():
            j = k - 4
            first = 2 * j + 8 * s
            partial(j).wait_recv()

            def block(b, carry):
                slot = first + b // NY
                yb = lax.rem(b, NY)
                late = late_of(slot)
                rows = pl.ds(pl.multiple_of(b * 16, 16), 16)
                logits = mine[j, rows, :] + got[j, rows, :]
                small = jnp.exp(-jnp.abs(logits))
                soft = jnp.maximum(logits, 0.0) + jnp.log1p(small)
                pool[late, yb] += jnp.log1p(soft)
                top = jnp.where(logits >= 0.0, 1.0, small)
                slope = top / ((1.0 + small) * (1.0 + soft))
                slopes[slot, yb] = slope.astype(jnp.bfloat16)
                return carry

            lax.fori_loop(0, 2 * NY, block, 0)
            slope_copy(j, first).start()

        return carry

    lax.fori_loop(1, STEPS + 4, step, 0)

    lane = lax.broadcasted_iota(jnp.int32, (NQ, LANES), 1)
    row = lax.broadcasted_iota(jnp.int32, (NQ, LANES), 0)
    for c in inputs[2:]:
        c.wait()
    query = queries[...].astype(jnp.float32)
    terms = jnp.zeros((NQ, LANES), jnp.float32)
    for late in range(2):
        for yb in range(NY):
            for m in range(2):
                total = jnp.sum(pool[late, yb, m * 8 : (m + 1) * 8, :], axis=0, keepdims=True)
                term = jnp.sum(query * total, axis=1, keepdims=True)
                terms = jnp.where(lane == m * 8 + yb * 2 + late, term, terms)

    def transpose(c, carry):
        at = pl.multiple_of(c * LANES, LANES)
        block = xs[:, :, :, pl.ds(at, LANES)].reshape(TOKENS, LANES)
        xt[pl.ds(at, LANES), :] = block.T
        return carry

    ar0[...] = terms
    to_core = copy(ar0, ar1, a1_s, a1_r, dev(ds=1))
    to_core.start()
    to_core.wait_recv()
    chip = terms + ar1[...]
    ar0_xy = ar2.at[x * NY + y]
    ar2[x * NY + y] = chip

    def to_xy(i):
        return copy(ar0_xy, ar0_xy, a2_s.at[i], a2_r.at[i], dev(dx=i // NY, dy=lax.rem(i, NY)))

    def from_xy(i):
        ref = ar2.at[wrap(x - i // NY, NX) * NY + wrap(y - lax.rem(i, NY), NY)]
        return copy(ref, ref, a2_s.at[i], a2_r.at[i], dev())

    def start_xy(i, carry):
        to_xy(i).start()
        return carry

    def wait_xy(i, carry):
        from_xy(i).wait_recv()
        return carry

    lax.fori_loop(1, NX * NY, start_xy, 0)
    lax.fori_loop(0, 6, transpose, 0)
    lax.fori_loop(1, NX * NY, wait_xy, 0)
    plane = jnp.zeros((NQ, LANES), jnp.float32)
    for i in range(NX * NY):
        plane += ar2[i]
    ar3[z] = plane
    ar_z = ar3.at[z]

    def to_z(i):
        return copy(ar_z, ar_z, a3_s.at[i], a3_r.at[i], dev(dz=i))

    def from_z(i):
        ref = ar3.at[wrap(z - i, NZ)]
        return copy(ref, ref, a3_s.at[i], a3_r.at[i], dev())

    def start_z(i, carry):
        to_z(i).start()
        return carry

    def wait_z(i, carry):
        from_z(i).wait_recv()
        return carry

    lax.fori_loop(1, NZ, start_z, 0)
    lax.fori_loop(6, DH // LANES, transpose, 0)

    for d in range(2):
        for c in ring_first(d) + ring_middle(d, 2) + ring_middle(d, 3) + ring_last(d):
            c.wait_send()
    for o in range(1, NY):
        own_y(o, y).wait_send()
        for i in range(1, 2 * STEPS + 1):
            n = 1 if i == 2 * STEPS else 2
            relay_x(i, o, 0, n).wait_send()
            relay_y(i, o, 0, n, y).wait_send()
    for k in range(STEPS):
        slope_copy(k, 2 * k + 8 * (1 - s)).wait_recv()
        slope_copy(k, 2 * k + 8 * s).wait_send()
        partial(k).wait_send()
    for i, (dx, ds) in enumerate(near):
        p1(i, dx, ds, 0).wait_send()
    to_core.wait_send()

    def sent_xy(i, carry):
        to_xy(i).wait_send()
        return carry

    lax.fori_loop(1, NX * NY, sent_xy, 0)
    lax.fori_loop(1, NZ, wait_z, 0)
    whole = jnp.zeros((NQ, LANES), jnp.float32)
    for i in range(NZ):
        whole += ar3[i]

    masks = []
    first = jnp.int32(0)
    scores = jnp.zeros((NQ, LANES), jnp.float32)
    for d in range(NDOC):
        after = first + doc_spans[d]
        masks.append((lane >= first) & (lane < after))
        term = jnp.sum(jnp.where(masks[d], whole, 0.0), axis=1, keepdims=True)
        scores = jnp.where(lane == d, term, scores)
        first = after
    scores = scores * (1.0 / (math.sqrt(VOCAB) * SPAN))
    valid = lane < NDOC
    row_top = jnp.max(jnp.where(valid, scores, -jnp.inf), axis=1, keepdims=True)
    total = jnp.sum(jnp.where(valid, jnp.exp(scores - row_top), 0.0), axis=1, keepdims=True)
    log_total = row_top + jnp.log(total)
    picks = jnp.zeros((NQ, LANES), jnp.float32)
    for q in range(NQ):
        picks = jnp.where((row == q) & (lane == labels[q]), 1.0, picks)
    picked = jnp.sum(scores * picks, axis=1, keepdims=True)
    loss[...] = jnp.sum(log_total - picked, axis=0, keepdims=True)
    grad = jnp.where(valid, jnp.exp(scores - log_total), 0.0) - picks
    grad = grad * (1.0 / math.sqrt(TOKENS))
    by_span = jnp.zeros((NQ, LANES), jnp.float32)
    for d in range(NDOC):
        column = jnp.sum(jnp.where(lane == d, grad, 0.0), axis=1, keepdims=True)
        by_span = jnp.where(masks[d], column, by_span)
    for i in range(SPANS):
        m, yb, late = i // 8, i // 2 % NY, i % 2
        spg[late, 2 * yb + m : 2 * yb + m + 1, :] = jnp.sum(
            by_span[:, i : i + 1] * query, axis=0, keepdims=True
        )

    def to_lg(slot, carry):
        factors = spg[late_of(slot)]
        for yb in range(NY):
            slope = slopes[slot, yb].astype(jnp.float32)
            parts = [
                slope[m * 8 : (m + 1) * 8] * factors[2 * yb + m : 2 * yb + m + 1] for m in range(2)
            ]
            at = pl.multiple_of(slot * 64 + yb * 16, 16)
            lg[pl.ds(at, 16), :] = jnp.concatenate(parts, axis=0).astype(jnp.bfloat16)
        return carry

    lax.fori_loop(0, NZ, to_lg, 0)

    def out_copy(b):
        here = pl.ds(pl.multiple_of(b * WQ, WQ), WQ)
        quarter = C_AT // WQ + wrap(x + b - C_AT // WQ, NX)
        at = pl.multiple_of(jnp.where(b < C_AT // WQ, b, quarter) * WQ, WQ)
        return pltpu.make_async_copy(outs.at[here], out.at[pl.ds(at, WQ)], o_sem.at[b])

    def to_out(b, carry):
        here = pl.ds(pl.multiple_of(b * WQ, WQ), WQ)
        block = jnp.dot(xt[here, :], lg[...], preferred_element_type=jnp.float32)
        outs[here, :] = block.astype(jnp.bfloat16)
        out_copy(b).start()
        return carry

    lax.fori_loop(0, DH // WQ, to_out, 0)

    def sent_z(i, carry):
        to_z(i).wait_send()
        return carry

    lax.fori_loop(1, NZ, sent_z, 0)

    def out_wait(b, carry):
        out_copy(b).wait()
        return carry

    lax.fori_loop(0, DH // WQ, out_wait, 0)


def shards(hidden, gain, head, queries, doc_spans, labels):
    dma = pltpu.SemaphoreType.DMA
    f32, bf16 = jnp.float32, jnp.bfloat16
    vmem = pl.BlockSpec(memory_space=pltpu.VMEM)
    hbm = pl.BlockSpec(memory_space=pltpu.HBM)
    grad_head, loss = pl.pallas_call(
        kernel,
        name="splade_head",
        out_shape=(
            jax.ShapeDtypeStruct((DH, V_DEV), bf16),
            jax.ShapeDtypeStruct((1, 1), f32),
        ),
        in_specs=[hbm] * 6,
        out_specs=(hbm, vmem),
        scratch_shapes=[
            pltpu.VMEM((1, 2, D), bf16),
            pltpu.VMEM((1, D), f32),
            pltpu.VMEM((NQ, V_DEV), bf16),
            pltpu.SMEM((NDOC,), jnp.int32),
            pltpu.SMEM((NQ,), jnp.int32),
            pltpu.VMEM((2, 2, 16, LANES), f32),
            pltpu.VMEM((16, 16, LANES), f32),
            pltpu.VMEM((NZ, NY, 16, DH), bf16),
            pltpu.VMEM((DH, V_DEV), bf16),
            pltpu.VMEM((STEPS, ROWS, V_DEV), f32),
            pltpu.VMEM((STEPS, ROWS, V_DEV), f32),
            pltpu.VMEM((STEPS, ROWS, V_DEV), f32),
            pltpu.VMEM((NZ, NY, 16, V_DEV), bf16),
            pltpu.VMEM((2, NY, 16, V_DEV), f32),
            pltpu.VMEM((DH, TOKENS), bf16),
            pltpu.VMEM((TOKENS, V_DEV), bf16),
            pltpu.VMEM((DH, V_DEV), bf16),
            pltpu.VMEM((2, 8, V_DEV), f32),
            pltpu.VMEM((NQ, LANES), f32),
            pltpu.VMEM((NQ, LANES), f32),
            pltpu.VMEM((NX * NY, NQ, LANES), f32),
            pltpu.VMEM((NZ, NQ, LANES), f32),
            dma((5,)), dma((5,)), dma((DH // WQ,)),
            dma((7,)), dma((7,)),
            dma((9, 3)), dma((9, 3)),
            dma((20,)), dma((20,)),
            dma((9, 3)), dma((9, 3)),
            dma((STEPS,)), dma((STEPS,)),
            dma((STEPS,)), dma((STEPS,)),
            dma, dma,
            dma((16,)), dma((16,)),
            dma((16,)), dma((16,)),
        ],
        compiler_params=pltpu.CompilerParams(
            collective_id=0, has_side_effects=True, vmem_limit_bytes=67_000_000
        ),
    )(hidden, gain.reshape(1, D), head, queries, doc_spans, labels)
    return (grad_head, loss.reshape(()))


def solution(mesh):
    return jax.shard_map(
        shards,
        mesh=mesh,
        in_specs=(
            P("segment", ("dp", "mp"), None),
            P(),
            P("segment", ("dp", "mp")),
            P(None, ("dp", "mp")),
            P(),
            P(),
        ),
        out_specs=(P("segment", ("dp", "mp")), P()),
        check_vma=False,
    )
```

time: 94.2 us -> 85.3 us (0.906)
  Pallas kernels: 84.4 us -> 79.2 us
  local copies, waits for them, and re-layouts: 6.35 us -> 3.05 us
    pallas_call x1, Pallas kernels: 84.4 us -> 79.2 us  [shards(): pl.pallas_call(kernel, name='splade_head', out_shape=(jax.ShapeDtypeStruc...]
    unnamed x13 -> x1, local copies, waits for them, and re-layouts: 6.35 us -> 3.05 us
where the time goes in v2:
time: 85.3 us; the launch traced here: 84.6 us
  Pallas kernels  79.2 us (93%)
  local copies, waits for them, and re-layouts  3.05 us (4%)
  between operations  2.38 us (3%)
    pallas_call x1, Pallas kernels, shards(): pl.pallas_call(kernel, name='splade_head', out_shape=(jax.ShapeDtypeStruc...  79.2 us
    unnamed x1, local copies, waits for them, and re-layouts  3.05 us

profile of v2, /device:TPU:1, one launch (start us, length us, event | category | flops | bytes accessed | tf_op | source)
XLA Modules:
  0.0 84.6 jit_solution(10589981196109184960)
XLA Ops:
  0.6 79.2 %splade_head.1 = (bf16[2048,512]{1,0:T(8,128)(2,1)}, f32[1,1]{1,0:T(1,128)}) custom-call(bf16[1,2,4096]{2,1,0:T(2,128)(2,1)} %hidden_at.1, f32[1,4096]{1,0:T(1,128)} %bitcast.2, bf16[2048,512]{1,0:T(8,128)(2,1)} %head.1, bf16[8,512]{1,0:T(8,128)(2,1)} %queries_at.1, s32[8]{0:T(128)} %doc_spans_at.1, s32[8]{0:T(128)} %labels_at.1), custom_call_target="tpu_custom_call" | custom-call | tf_op jit(solution)/shard_map/splade_head/pallas_call | solution.py:479
  79.8 3.0 %copy.10 = bf16[2048,512]{1,0:T(8,128)(2,1)} copy(bf16[2048,512]{1,0:T(8,128)(2,1)} %get-tuple-element.8) | data formatting | bytes 4194304

commit v3 on v2

--- a/solution.py
+++ b/solution.py
@@ -32,8 +32,11 @@
 STEPS = 4
 
 
-def wrap(i, n):
-    return lax.rem(i + 2 * n, n)
+def around(at, by, n):
+    by %= n
+    if by == 0:
+        return at
+    return jnp.where(at >= n - by, at + (by - n), at + by)
 
 
 def kernel(
@@ -52,12 +55,13 @@
     y = dp // NZ
     z = lax.rem(dp, NZ)
 
+    xs_of = [around(x, i, NX) for i in range(NX)]
+    ys_of = [around(y, i, NY) for i in range(NY)]
+    zs_of = [around(z, i, NZ) for i in range(NZ)]
+    ss_of = [s, 1 - s]
+
     def dev(dx=0, dy=0, dz=0, ds=0):
-        return (
-            wrap(y + dy, NY) * NZ + wrap(z + dz, NZ),
-            wrap(s + ds, 2),
-            wrap(x + dx, NX),
-        )
+        return (ys_of[dy % NY] * NZ + zs_of[dz % NZ], ss_of[ds], xs_of[dx % NX])
 
     def copy(src, dst, s_sem, r_sem, device):
         return pltpu.make_async_remote_copy(
@@ -84,7 +88,7 @@
 
     h_copies = [pltpu.make_async_copy(head.at[pl.ds(0, C_AT)], hs.at[pl.ds(0, C_AT)], h_sem.at[0])]
     for r in range(NX):
-        at = pl.multiple_of(C_AT + wrap(x + r, NX) * WQ, WQ)
+        at = pl.multiple_of(C_AT + xs_of[r] * WQ, WQ)
         h_copies.append(
             pltpu.make_async_copy(
                 head.at[pl.ds(at, WQ)], hs.at[pl.ds(C_AT + r * WQ, WQ)], h_sem.at[1 + r]
@@ -104,7 +108,7 @@
 
     def p1(i, dx, ds, landing):
         return copy(
-            ysend.at[wrap(s + ds, 2)],
+            ysend.at[ss_of[ds]],
             yland.at[pl.ds(landing * 2, 2)],
             p1_s.at[i], p1_r.at[i], dev(dx=dx, ds=ds),
         )
@@ -116,7 +120,7 @@
     yland[pl.ds((s * NX + x) * 2, 2)] = ysend[s]
     pool[...] = jnp.zeros_like(pool)
     for i, (dx, ds) in enumerate(near):
-        p1(i, dx, ds, wrap(s + ds, 2) * NX + wrap(x - dx, NX)).wait_recv()
+        p1(i, dx, ds, ss_of[ds] * NX + xs_of[-dx % NX]).wait_recv()
     for k in range(C_AT // LANES):
         xs[OWN, y, :, k * LANES : (k + 1) * LANES] = yland[:, k, :].astype(jnp.bfloat16)
     for xx in range(NX):
@@ -181,8 +185,9 @@
         off = jnp.where(slot < 8, NZ - 1 - slot, jnp.where(slot == OWN, 0, slot - 7))
         return jnp.where(lax.rem(z + off, NZ) >= NZ // 2, 1, 0)
 
-    def rows_of(slot):
-        return xs[pl.ds(slot, 2)].reshape(ROWS, DH)
+    def term(slot, at, end):
+        rows = xs[pl.ds(slot, 2), :, :, at:end].reshape(ROWS, end - at)
+        return jnp.dot(rows, hs[at:end, :], preferred_element_type=jnp.float32)
 
     for d in range(2):
         start(ring_first(d))
@@ -242,22 +247,11 @@
 
                 def y_to_x(first, n, d=d):
                     for dy in range(1, NY):
-                        relay_y(2 * j - 1 + d, dy, first, n, wrap(y - dy, NY)).wait_recv()
+                        relay_y(2 * j - 1 + d, dy, first, n, ys_of[-dy % NY]).wait_recv()
                     for dx in range(1, NX):
                         relay_x(2 * j - 1 + d, dx, first, n).start()
 
                 whole_or_not(j, d, y_to_x)
-
-        @pl.when((k >= 3) & (k <= STEPS + 2))
-        def _():
-            j = k - 2
-            for d in range(2):
-
-                def from_x(first, n, d=d):
-                    for dx in range(1, NX):
-                        relay_x(2 * j - 1 + d, dx, first, n).wait_recv()
-
-                whole_or_not(j, d, from_x)
 
             @pl.when(j == 1)
             def _():
@@ -267,14 +261,27 @@
             @pl.when(j == STEPS)
             def _():
                 for dy in range(1, NY):
-                    own_y(dy, wrap(y - dy, NY)).wait_recv()
+                    own_y(dy, ys_of[-dy % NY]).wait_recv()
 
             first = 2 * (j - 1)
-            other = rows_of(first + 8 * (1 - s))
-            sent[j - 1] = jnp.dot(other, hs[...], preferred_element_type=jnp.float32)
+            sent[j - 1] = term(first + 8 * (1 - s), 0, WB + WQ)
+            mine[j - 1] = term(first + 8 * s, 0, WB + WQ)
+
+        @pl.when((k >= 3) & (k <= STEPS + 2))
+        def _():
+            j = k - 2
+            for d in range(2):
+
+                def from_x(first, n, d=d):
+                    for dx in range(1, NX):
+                        relay_x(2 * j - 1 + d, dx, first, n).wait_recv()
+
+                whole_or_not(j, d, from_x)
+
+            first = 2 * (j - 1)
+            sent[j - 1] += term(first + 8 * (1 - s), WB + WQ, DH)
             partial(j - 1).start()
-            own = rows_of(first + 8 * s)
-            mine[j - 1] = jnp.dot(own, hs[...], preferred_element_type=jnp.float32)
+            mine[j - 1] += term(first + 8 * s, WB + WQ, DH)
 
         @pl.when(k >= 4)
         def _():
@@ -282,21 +289,22 @@
             first = 2 * j + 8 * s
             partial(j).wait_recv()
 
-            def block(b, carry):
-                slot = first + b // NY
-                yb = lax.rem(b, NY)
+            for o in range(2):
+                slot = first + o
                 late = late_of(slot)
-                rows = pl.ds(pl.multiple_of(b * 16, 16), 16)
-                logits = mine[j, rows, :] + got[j, rows, :]
-                small = jnp.exp(-jnp.abs(logits))
-                soft = jnp.maximum(logits, 0.0) + jnp.log1p(small)
-                pool[late, yb] += jnp.log1p(soft)
-                top = jnp.where(logits >= 0.0, 1.0, small)
-                slope = top / ((1.0 + small) * (1.0 + soft))
-                slopes[slot, yb] = slope.astype(jnp.bfloat16)
-                return carry
-
-            lax.fori_loop(0, 2 * NY, block, 0)
+
+                def block(yb, carry, o=o, slot=slot, late=late):
+                    rows = pl.ds(pl.multiple_of(o * 64 + yb * 16, 16), 16)
+                    logits = mine[j, rows, :] + got[j, rows, :]
+                    small = jnp.exp(-jnp.abs(logits))
+                    soft = jnp.maximum(logits, 0.0) + jnp.log1p(small)
+                    pool[late, yb] += jnp.log1p(soft)
+                    top = jnp.where(logits >= 0.0, 1.0, small)
+                    slope = top / ((1.0 + small) * (1.0 + soft))
+                    slopes[slot, yb] = slope.astype(jnp.bfloat16)
+                    return carry
+
+                lax.fori_loop(0, NY, block, 0)
             slope_copy(j, first).start()
 
         return carry
@@ -330,24 +338,22 @@
     ar0_xy = ar2.at[x * NY + y]
     ar2[x * NY + y] = chip
 
-    def to_xy(i):
-        return copy(ar0_xy, ar0_xy, a2_s.at[i], a2_r.at[i], dev(dx=i // NY, dy=lax.rem(i, NY)))
-
-    def from_xy(i):
-        ref = ar2.at[wrap(x - i // NY, NX) * NY + wrap(y - lax.rem(i, NY), NY)]
-        return copy(ref, ref, a2_s.at[i], a2_r.at[i], dev())
-
-    def start_xy(i, carry):
-        to_xy(i).start()
-        return carry
-
-    def wait_xy(i, carry):
-        from_xy(i).wait_recv()
-        return carry
-
-    lax.fori_loop(1, NX * NY, start_xy, 0)
+    plane_peers = [(dx, dy) for dx in range(NX) for dy in range(NY) if dx or dy]
+
+    def to_xy(dx, dy):
+        i = dx * NY + dy
+        return copy(ar0_xy, ar0_xy, a2_s.at[i], a2_r.at[i], dev(dx=dx, dy=dy))
+
+    def from_xy(dx, dy):
+        i = dx * NY + dy
+        ref = ar2.at[xs_of[-dx % NX] * NY + ys_of[-dy % NY]]
+        return copy(ref, ref, a2_s.at[i], a2_r.at[i], dev(dx=dx, dy=dy))
+
+    for dx, dy in plane_peers:
+        to_xy(dx, dy).start()
     lax.fori_loop(0, 6, transpose, 0)
-    lax.fori_loop(1, NX * NY, wait_xy, 0)
+    for dx, dy in plane_peers:
+        from_xy(dx, dy).wait_recv()
     plane = jnp.zeros((NQ, LANES), jnp.float32)
     for i in range(NX * NY):
         plane += ar2[i]
@@ -358,18 +364,11 @@
         return copy(ar_z, ar_z, a3_s.at[i], a3_r.at[i], dev(dz=i))
 
     def from_z(i):
-        ref = ar3.at[wrap(z - i, NZ)]
-        return copy(ref, ref, a3_s.at[i], a3_r.at[i], dev())
-
-    def start_z(i, carry):
+        ref = ar3.at[zs_of[-i % NZ]]
+        return copy(ref, ref, a3_s.at[i], a3_r.at[i], dev(dz=i))
+
+    for i in range(1, NZ):
         to_z(i).start()
-        return carry
-
-    def wait_z(i, carry):
-        from_z(i).wait_recv()
-        return carry
-
-    lax.fori_loop(1, NZ, start_z, 0)
     lax.fori_loop(6, DH // LANES, transpose, 0)
 
     for d in range(2):
@@ -389,12 +388,10 @@
         p1(i, dx, ds, 0).wait_send()
     to_core.wait_send()
 
-    def sent_xy(i, carry):
-        to_xy(i).wait_send()
-        return carry
-
-    lax.fori_loop(1, NX * NY, sent_xy, 0)
-    lax.fori_loop(1, NZ, wait_z, 0)
+    for dx, dy in plane_peers:
+        to_xy(dx, dy).wait_send()
+    for i in range(1, NZ):
+        from_z(i).wait_recv()
     whole = jnp.zeros((NQ, LANES), jnp.float32)
     for i in range(NZ):
         whole += ar3[i]
@@ -445,7 +442,7 @@
 
     def out_copy(b):
         here = pl.ds(pl.multiple_of(b * WQ, WQ), WQ)
-        quarter = C_AT // WQ + wrap(x + b - C_AT // WQ, NX)
+        quarter = C_AT // WQ + lax.rem(x + jnp.maximum(b - C_AT // WQ, 0), NX)
         at = pl.multiple_of(jnp.where(b < C_AT // WQ, b, quarter) * WQ, WQ)
         return pltpu.make_async_copy(outs.at[here], out.at[pl.ds(at, WQ)], o_sem.at[b])
 
@@ -458,11 +455,8 @@
 
     lax.fori_loop(0, DH // WQ, to_out, 0)
 
-    def sent_z(i, carry):
+    for i in range(1, NZ):
         to_z(i).wait_send()
-        return carry
-
-    lax.fori_loop(1, NZ, sent_z, 0)
 
     def out_wait(b, carry):
         out_copy(b).wait()

time: 85.3 us -> 84.9 us (level)
  no operation moved by 1% of the time
where the time goes in v3:
time: 84.9 us; the launch traced here: 84.1 us
  Pallas kernels  78.7 us (93%)
  local copies, waits for them, and re-layouts  3.05 us (4%)
  between operations  2.38 us (3%)
    pallas_call x1, Pallas kernels, shards(): pl.pallas_call(kernel, name='splade_head', out_shape=(jax.ShapeDtypeStruc...  78.7 us
    unnamed x1, local copies, waits for them, and re-layouts  3.05 us

profile of v3, /device:TPU:1, one launch (start us, length us, event | category | flops | bytes accessed | tf_op | source)
XLA Modules:
  0.0 84.1 jit_solution(15239398375361138509)
XLA Ops:
  0.6 78.7 %splade_head.1 = (bf16[2048,512]{1,0:T(8,128)(2,1)}, f32[1,1]{1,0:T(1,128)}) custom-call(bf16[1,2,4096]{2,1,0:T(2,128)(2,1)} %hidden_at.1, f32[1,4096]{1,0:T(1,128)} %bitcast.2, bf16[2048,512]{1,0:T(8,128)(2,1)} %head.1, bf16[8,512]{1,0:T(8,128)(2,1)} %queries_at.1, s32[8]{0:T(128)} %doc_spans_at.1, s32[8]{0:T(128)} %labels_at.1), custom_call_target="tpu_custom_call" | custom-call | tf_op jit(solution)/shard_map/splade_head/pallas_call | solution.py:473
  79.4 3.0 %copy.10 = bf16[2048,512]{1,0:T(8,128)(2,1)} copy(bf16[2048,512]{1,0:T(8,128)(2,1)} %get-tuple-element.8) | data formatting | bytes 4194304
